TPU v7x, 512 devices: a whole 4x4x16 slice. The times are simulated.
512 devices in a mesh: grp: 4 (over z_hi, core), seq: 128 (over x, y, z_lo).
Axes of the slice: x: 4, y: 4, z: 16 (z_hi: 2, z_lo: 8; z = z_hi * 8 + z_lo), core: 2. Of those that a mesh axis runs over, the one named last changes fastest.
Arguments:
- cand_queries: bfloat16 [4096, 128, 128], P(('grp', 'seq')), may hold values from -256 to 256
- candidate_keys: bfloat16 [512, 128, 128], P(('grp', 'seq')), may hold values from -6 to 6
- candidate_values: bfloat16 [512, 128, 128], P(('grp', 'seq')), may hold values from -24 to 24
- prefix_rotated_keys: bfloat16 [2048, 1024], P(('grp', 'seq')), may hold values from -6.1 to 6.1
- prefix_value_matrix: bfloat16 [2048, 1024], P(('grp', 'seq')), may hold values from -24 to 24
- lengths: int32 [64], replicated, may hold values from 32 to 128
Outputs:
- attended: bfloat16 [4096, 128, 128], P(('grp', 'seq'))
All inputs are finite; a program needn't handle non-finite values.
Results may differ from a plain program's by a relative error of at most 0.0076.
Values may be sent and summed in bfloat16 or wider, within the bound.
A program may use at most 64 MiB of HBM per device.

v0:
```python
import math
import jax
import jax.numpy as jnp
import numpy as np
from jax import lax
from jax.sharding import PartitionSpec as P

QUERY_HEADS = 64
KEY_VALUE_HEADS = 8
HEAD_WIDTH = 128
rope_base = 500000.0


def in_one_piece(arrays, axis, dim, along):
    both = jnp.concatenate(arrays, axis=along)
    filled, at, outs = (lax.all_gather(both, axis, axis=dim, tiled=True), 0, [])
    for a in arrays:
        outs.append(lax.slice_in_dim(filled, at, at + a.shape[along], axis=along))
        at += a.shape[along]
    return tuple(outs)


def rotate(vectors, positions):
    half_width = vectors.shape[-1] // 2
    exponents = jnp.arange(half_width, dtype=jnp.float32) * (2.0 / vectors.shape[-1])
    frequency = 1.0 / jnp.power(jnp.float32(rope_base), exponents)
    angles = positions.astype(jnp.float32)[:, None] * frequency[None, :]
    cosine = jnp.cos(angles)
    sine_table = jnp.sin(angles)
    lower_half = vectors[..., :half_width]
    upper_half = vectors[..., half_width:]
    return jnp.concatenate(
        [
            lower_half * cosine - upper_half * sine_table,
            upper_half * cosine + lower_half * sine_table,
        ],
        axis=-1,
    )


def pick_heads(key_row_list, value_row_list, head_table, sequence_count):
    row_total = key_row_list.shape[0]
    stacked = jnp.stack(
        [
            key_row_list.reshape(row_total, KEY_VALUE_HEADS, HEAD_WIDTH),
            value_row_list.reshape(row_total, KEY_VALUE_HEADS, HEAD_WIDTH),
        ],
        axis=2,
    )
    picked = jnp.take(stacked, head_table, axis=1)
    return picked.reshape(row_total, sequence_count, -1).transpose(1, 0, 2)


def shards(
    cand_queries,
    candidate_keys,
    candidate_values,
    prefix_rotated_keys,
    prefix_value_matrix,
    lengths,
):
    sequence_count = lax.axis_size("seq")
    grp_count = lax.axis_size("grp")
    head_rows = cand_queries.shape[0]
    cand_length = cand_queries.shape[1]
    key_value_rows = candidate_keys.shape[0]
    group_width = QUERY_HEADS // KEY_VALUE_HEADS
    key_value_heads = min(KEY_VALUE_HEADS, key_value_rows)
    prefix_here = prefix_rotated_keys.shape[0]
    prefix_total = prefix_here * sequence_count * grp_count
    score_scale = 1.0 / math.sqrt(HEAD_WIDTH)
    prefix_pick = (
        (np.arange(sequence_count)[:, None] * key_value_rows + np.arange(key_value_heads)[None, :])
        % KEY_VALUE_HEADS
    ).reshape(-1)
    copies = in_one_piece((prefix_rotated_keys, prefix_value_matrix), "grp", 0, 1)
    outgoing = pick_heads(copies[0], copies[1], prefix_pick, sequence_count)
    prefix_pair = lax.all_to_all(outgoing, "seq", split_axis=0, concat_axis=1, tiled=True)
    prefix_pair = prefix_pair.reshape(prefix_total, key_value_heads, 2, HEAD_WIDTH)
    kv_table = np.arange(key_value_rows) % key_value_heads
    prefix_key_rows = jnp.take(prefix_pair[:, :, 0], kv_table, axis=1).transpose(1, 0, 2)
    prefix_value_rows = jnp.take(prefix_pair[:, :, 1], kv_table, axis=1).transpose(1, 0, 2)
    positions = prefix_total + jnp.arange(cand_length, dtype=jnp.int32)
    new_keys = rotate(candidate_keys.astype(jnp.float32), positions).astype(jnp.bfloat16)
    rotated = rotate(cand_queries.astype(jnp.float32), positions).astype(jnp.bfloat16)
    rotated = rotated.reshape(key_value_rows, group_width * cand_length, HEAD_WIDTH)
    all_keys = jnp.concatenate([prefix_key_rows, new_keys], axis=1)
    all_values = jnp.concatenate([prefix_value_rows, candidate_values], axis=1)
    key_count = prefix_total + cand_length
    block_rows = math.gcd(key_count, 512)
    block_count = key_count // block_rows
    row_total = group_width * cand_length
    row_token = jnp.arange(row_total, dtype=jnp.int32) % cand_length
    starts = jnp.arange(block_count, dtype=jnp.int32) * block_rows

    def attend(carry, block):
        maxima, totals, weighted = carry
        block_keys, block_values, first_row = block
        scores = (
            jnp.einsum("krd,knd->krn", rotated, block_keys, preferred_element_type=jnp.float32)
            * score_scale
        )
        cand_offset = first_row + jnp.arange(block_rows, dtype=jnp.int32) - prefix_total
        scores = jnp.where((cand_offset[None, :] <= row_token[:, None])[None], scores, -jnp.inf)
        highest = jnp.maximum(maxima, jnp.max(scores, axis=-1))
        decline = jnp.exp(maxima - highest)
        exponent = jnp.exp(scores - highest[..., None])
        totals = totals * decline + jnp.sum(exponent, axis=-1)
        weighted = weighted * decline[..., None] + jnp.einsum(
            "krn,knd->krd",
            exponent.astype(jnp.bfloat16),
            block_values,
            preferred_element_type=jnp.float32,
        )
        return ((highest, totals, weighted), None)

    start_state = (
        jnp.full((key_value_rows, row_total), -1e30, jnp.float32),
        jnp.zeros((key_value_rows, row_total), jnp.float32),
        jnp.zeros((key_value_rows, row_total, HEAD_WIDTH), jnp.float32),
    )
    key_blocks = all_keys.reshape(key_value_rows, block_count, block_rows, HEAD_WIDTH).transpose(
        1, 0, 2, 3
    )
    value_blocks = all_values.reshape(
        key_value_rows, block_count, block_rows, HEAD_WIDTH
    ).transpose(1, 0, 2, 3)
    final_state, unused = lax.scan(attend, start_state, (key_blocks, value_blocks, starts))
    maxima, totals, weighted = final_state
    attended = (weighted / totals[..., None]).reshape(head_rows, cand_length, HEAD_WIDTH)
    device_place = lax.axis_index("grp") * sequence_count + lax.axis_index("seq")
    cand_of_row = (device_place * head_rows + jnp.arange(head_rows, dtype=jnp.int32)) // QUERY_HEADS
    cand_slots = jnp.arange(lengths.shape[0], dtype=jnp.int32)
    cand_limit = jnp.sum(
        jnp.where(cand_of_row[:, None] == cand_slots[None, :], lengths[None, :], 0), axis=1
    )
    visible = jnp.arange(cand_length, dtype=jnp.int32)[None, :] < cand_limit[:, None]
    return jnp.where(visible[:, :, None], attended, jnp.float32(0.0)).astype(jnp.bfloat16)


def solution(mesh):
    return jax.shard_map(
        shards,
        mesh=mesh,
        in_specs=(
            P(("grp", "seq"), None, None),
            P(("grp", "seq"), None, None),
            P(("grp", "seq"), None, None),
            P(("grp", "seq"), None),
            P(("grp", "seq"), None),
            P(),
        ),
        out_specs=P(("grp", "seq"), None, None),
        check_vma=False,
    )
```

profile of v0, /device:TPU:1, one launch (start us, length us, event | category | flops | bytes accessed | tf_op | source)
XLA Modules:
  0.0 135.4 jit_solution(17232865180039130087)
XLA Ops:
  0.0 0.7 maximum_bitcast_fusion
  0.7 20.7 %all-gather = bf16[4,4,2048]{2,1,0:T(4,128)(2,1)S(1)} all-gather(bf16[1,4,2048]{2,1,0:T(4,128)(2,1)S(1)} %maximum_bitcast_fusion), channel_id=1, replica_groups=mesh['grp'=4,'seq'=128] {'grp'}, dimensions={0}, use_global_device_ids=true | all-gather | bytes 81920 | tf_op jit(solution)/shard_map/all_gather | solution.py:16
  21.5 0.7 pad_clamp_fusion
  22.2 0.8 gather_fusion
  22.9 1.1 copy.33
  24.0 1.7 %copy.34 = bf16[128,16,256]{2,1,0:T(8,128)(2,1)} copy(bf16[128,16,256]{0,2,1:T(8,128)(2,1)S(1)} %bitcast.75) | data formatting | bytes 2097152 | tf_op jit(solution)/shard_map/transpose | solution.py:51
  25.7 14.3 %all-to-all-start = ((bf16[128,16,256]{2,1,0:T(8,128)(2,1)}), bf16[128,16,256]{2,1,0:T(8,128)(2,1)S(1)}, u32[]{:S(2)}, u32[]{:S(2)}) async-start(bf16[128,16,256]{2,1,0:T(8,128)(2,1)} %copy.34), calls=%async_computation | async-start | bytes 2097152 | tf_op jit(solution)/shard_map/all_to_all | solution.py:78
  41.7 52.1 %all-to-all-done = bf16[128,16,256]{2,1,0:T(8,128)(2,1)S(1)} async-done(((bf16[128,16,256]{2,1,0:T(8,128)(2,1)}), bf16[128,16,256]{2,1,0:T(8,128)(2,1)S(1)}, u32[]{:S(2)}, u32[]{:S(2)}) %all-to-all-start) | async-done | bytes 1048608 | tf_op jit(solution)/shard_map/all_to_all | solution.py:78
  94.1 1.5 %fusion.31 = (bf16[2048,1,1,128]{3,2,0,1:T(2,128)(2,1)S(1)}, bf16[2048,1,1,128]{3,2,0,1:T(2,128)(2,1)S(1)}) fusion(bf16[2048,1,2,128]{3,2,0,1:T(2,128)(2,1)S(1)} %reshape.324), kind=kLoop, calls=%fused_computation.69 | loop fusion | bytes 2097152 | tf_op jit(solution)/shard_map/slice | solution.py:82
  95.8 0.7 copy-done.1
  96.6 37.7 %while.17 = (s32[]{:T(128)}, f32[1,1024]{1,0:T(1,128)S(1)}, f32[1,1024]{1,0:T(1,128)S(1)}, f32[1,1024,128]{2,1,0:T(8,128)S(1)}, s32[17]{0:T(128)S(1)}, /*index=5...) while((s32[]{:T(128)}, f32[1,1024]{1,0:T(1,128)S(1)}, ...), condition=%wide.region_4.5_spmd.clone, body=%wide.region_1.4_spmd.clone.sunk | while | flops 68562176 | bytes 3024009 | solution.py:128
  96.6 0.7 dynamic_slice.38
  97.3 0.7 add_add_fusion.2
  98.8 0.7 dynamic_slice.38
  99.5 0.7 add_add_fusion.2
  101.0 0.7 dynamic_slice.38
  101.7 0.7 add_add_fusion.2
  102.8 0.4 fusion.45
  103.2 0.7 dynamic_slice.38
  103.9 0.7 add_add_fusion.2
  105.0 0.4 fusion.45
  105.5 0.7 dynamic_slice.38
  106.1 0.7 add_add_fusion.2
  107.7 0.7 dynamic_slice.38
  108.3 0.7 add_add_fusion.2
  109.9 0.7 dynamic_slice.38
  110.6 0.7 add_add_fusion.2
  112.1 0.7 dynamic_slice.38
  112.8 0.7 add_add_fusion.2
  114.3 0.7 dynamic_slice.38
  115.0 0.7 add_add_fusion.2
  116.5 0.7 dynamic_slice.38
  117.2 0.7 add_add_fusion.2
  118.7 0.7 dynamic_slice.38
  119.4 0.7 add_add_fusion.2
  121.0 0.7 dynamic_slice.38
  121.6 0.7 add_add_fusion.2
  123.2 0.7 dynamic_slice.38
  123.8 0.7 add_add_fusion.2
  125.4 0.7 dynamic_slice.38
  126.1 0.7 add_add_fusion.2
  127.6 0.7 dynamic_slice.38
  128.3 0.7 add_add_fusion.2
  129.8 0.7 dynamic_slice.38
  130.5 0.7 add_add_fusion.2
  132.0 0.7 dynamic_slice.38
  132.7 0.7 add_add_fusion.2
  134.5 0.9 select_convert_fusion
  (154 shorter events, 14.8 us)
Async XLA Ops:
  25.7 14.4 %copy-start = (bf16[8,128,128]{2,1,0:T(8,128)(2,1)S(1)}, bf16[8,128,128]{2,1,0:T(8,128)(2,1)}, u32[]{:S(2)}) copy-start(bf16[8,128,128]{2,1,0:T(8,128)(2,1)} %param.10) | copy-start | bytes 786436
  25.7 14.4 %copy-start.2 = (bf16[1,128,128]{2,1,0:T(8,128)(2,1)S(1)}, bf16[1,128,128]{2,1,0:T(8,128)(2,1)}, u32[]{:S(2)}) copy-start(bf16[1,128,128]{2,1,0:T(8,128)(2,1)} %param.11) | copy-start | bytes 98308
  25.7 68.1 %all-to-all-start = ((bf16[128,16,256]{2,1,0:T(8,128)(2,1)}), bf16[128,16,256]{2,1,0:T(8,128)(2,1)S(1)}, u32[]{:S(2)}, u32[]{:S(2)}) async-start(bf16[128,16,256]{2,1,0:T(8,128)(2,1)} %copy.34), calls=%async_computation | async-start | bytes 2097152 | tf_op jit(solution)/shard_map/all_to_all | solution.py:78
  40.1 0.7 copy-start.3
  95.8 0.8 copy-start.1
where the time goes:
time: 136 us; the launch traced here: 135 us
  waiting for transfers between devices  52.1 us (38%)
  blocking collectives  20.7 us (15%)
  other arithmetic  17.9 us (13%)
  local copies, waits for them, and re-layouts  17.9 us (13%)
  starting transfers between devices  14.3 us (11%)
  matrix products  11.1 us (8%)
    all_to_all x1, waiting for transfers between devices, shards(): lax.all_to_all(outgoing, 'seq', split_axis=0, concat_axis=1, tiled=True)  52.1 us
    all_gather x1, blocking collectives, in_one_piece(): filled, at, outs = (lax.all_gather(both, axis, axis=dim, tiled=True), 0, [])  20.7 us
    all_to_all x1, starting transfers between devices, shards(): lax.all_to_all(outgoing, 'seq', split_axis=0, concat_axis=1, tiled=True)  14.3 us
    sub x17, other arithmetic, attend(): first_row + jnp.arange(block_rows, dtype=jnp.int32) - prefix_total  11.8 us
    dynamic_slice x17, local copies, waits for them, and re-layouts, shards(): lax.scan(attend, start_state, (key_blocks, value_blocks, starts))  11.3 us
    dot_general x17, matrix products, attend(): jnp.einsum('krn,knd->krd', exponent.astype(jnp.bfloat16), block_values, p...  6.91 us
    dot_general x17, matrix products, attend(): jnp.einsum('krd,knd->krn', rotated, block_keys, preferred_element_type=jn...  4.16 us
  transfers between devices with their start and end apart: 1, of which 1 were waited for; matrix products, arithmetic and copies ran while one was open for 1% of the time, Pallas kernels for 0%

commit v1 on v0

--- a/solution.py
+++ b/solution.py
@@ -75,7 +75,10 @@
     ).reshape(-1)
     copies = in_one_piece((prefix_rotated_keys, prefix_value_matrix), "grp", 0, 1)
     outgoing = pick_heads(copies[0], copies[1], prefix_pick, sequence_count)
-    prefix_pair = lax.all_to_all(outgoing, "seq", split_axis=0, concat_axis=1, tiled=True)
+    prefix_pair = jnp.concatenate(
+        lax.all_to_all(jnp.stack(jnp.split(outgoing, lax.axis_size("seq"), axis=0)), "seq", 0, 0),
+        axis=1,
+    )
     prefix_pair = prefix_pair.reshape(prefix_total, key_value_heads, 2, HEAD_WIDTH)
     kv_table = np.arange(key_value_rows) % key_value_heads
     prefix_key_rows = jnp.take(prefix_pair[:, :, 0], kv_table, axis=1).transpose(1, 0, 2)

time: 136 us -> 293 us (2.15)
  local copies, waits for them, and re-layouts: 17.9 us -> 175 us
    split x0 -> x7, local copies, waits for them, and re-layouts: none -> 83.3 us  [shards(): jnp.split(outgoing, lax.axis_size('seq'), axis=0)]
    unnamed x14 -> x141, local copies, waits for them, and re-layouts: 1.03 us -> 76.4 us
where the time goes in v1:
time: 293 us
  local copies, waits for them, and re-layouts  175 us (60%)
  waiting for transfers between devices  52.1 us (18%)
  blocking collectives  20.7 us (7%)
  other arithmetic  17.9 us (6%)
  starting transfers between devices  14.3 us (5%)
  matrix products  11.1 us (4%)
    split x7, local copies, waits for them, and re-layouts, shards(): jnp.split(outgoing, lax.axis_size('seq'), axis=0)  83.3 us
    unnamed x141, local copies, waits for them, and re-layouts  76.4 us
    all_to_all x1, waiting for transfers between devices, shards(): lax.all_to_all(jnp.stack(jnp.split(outgoing, lax.axis_size('seq'), axis=0...  52.1 us
    all_gather x1, blocking collectives, in_one_piece(): filled, at, outs = (lax.all_gather(both, axis, axis=dim, tiled=True), 0, [])  20.7 us
    all_to_all x1, starting transfers between devices, shards(): lax.all_to_all(jnp.stack(jnp.split(outgoing, lax.axis_size('seq'), axis=0...  14.3 us
    sub x17, other arithmetic, attend(): first_row + jnp.arange(block_rows, dtype=jnp.int32) - prefix_total  11.8 us
    dynamic_slice x17, local copies, waits for them, and re-layouts, shards(): lax.scan(attend, start_state, (key_blocks, value_blocks, starts))  11.3 us
    dot_general x17, matrix products, attend(): jnp.einsum('krn,knd->krd', exponent.astype(jnp.bfloat16), block_values, p...  6.91 us
  transfers between devices with their start and end apart: 1, of which 1 were waited for; matrix products, arithmetic and copies ran while one was open for 1% of the time, Pallas kernels for 0%

profile of v1, /device:TPU:1, one launch (start us, length us, event | category | flops | bytes accessed | tf_op | source)
XLA Modules:
  0.0 293.0 jit_solution(2975652573965990210)
XLA Ops:
  0.0 0.7 maximum_bitcast_fusion
  0.7 20.7 %all-gather = bf16[4,4,2048]{2,1,0:T(4,128)(2,1)S(1)} all-gather(bf16[1,4,2048]{2,1,0:T(4,128)(2,1)S(1)} %maximum_bitcast_fusion), channel_id=1, replica_groups=mesh['grp'=4,'seq'=128] {'grp'}, dimensions={0}, use_global_device_ids=true | all-gather | bytes 81920 | tf_op jit(solution)/shard_map/all_gather | solution.py:16
  22.2 0.8 gather_fusion
  22.9 1.1 copy.3646
  24.0 8.7 %slice_reduce_fusion.114 = (bf16[16,256]{1,0:T(8,128)(2,1)S(1)}, bf16[16,256]{1,0:T(8,128)(2,1)S(1)}, bf16[16,256]{1,0:T(8,128)(2,1)S(1)}, bf16[16,256]{1,0:T(8,...) fusion(bf16[128,16,256]{0,2,1:T(8,128)(2,1)S(1)} %bitcast.332), kind=kLoop, calls=%fused_computation.145 | loop fusion | bytes 229376 | tf_op jit(solution)/shard_map/split | solution.py:79
  32.8 12.4 %slice_reduce_fusion.95 = (bf16[16,256]{1,0:T(8,128)(2,1)S(1)}, bf16[16,256]{1,0:T(8,128)(2,1)S(1)}, bf16[16,256]{1,0:T(8,128)(2,1)S(1)}, bf16[16,256]{1,0:T(8,1...) fusion(bf16[128,16,256]{0,2,1:T(8,128)(2,1)S(1)} %bitcast.333), kind=kLoop, calls=%fused_computation.126 | loop fusion | bytes 311296 | tf_op jit(solution)/shard_map/split | solution.py:79
  45.1 12.4 %slice_reduce_fusion.76 = (bf16[16,256]{1,0:T(8,128)(2,1)S(1)}, bf16[16,256]{1,0:T(8,128)(2,1)S(1)}, bf16[16,256]{1,0:T(8,128)(2,1)S(1)}, bf16[16,256]{1,0:T(8,1...) fusion(bf16[128,16,256]{0,2,1:T(8,128)(2,1)S(1)} %bitcast.334), kind=kLoop, calls=%fused_computation.107 | loop fusion | bytes 311296 | tf_op jit(solution)/shard_map/split | solution.py:79
  57.5 12.5 %slice_reduce_fusion.57 = (bf16[16,256]{1,0:T(8,128)(2,1)S(1)}, bf16[16,256]{1,0:T(8,128)(2,1)S(1)}, bf16[16,256]{1,0:T(8,128)(2,1)S(1)}, bf16[16,256]{1,0:T(8,1...) fusion(bf16[128,16,256]{0,2,1:T(8,128)(2,1)S(1)} %bitcast.335), kind=kLoop, calls=%fused_computation.88 | loop fusion | bytes 311296 | tf_op jit(solution)/shard_map/split | solution.py:79
  70.0 12.4 %slice_reduce_fusion.38 = (bf16[16,256]{1,0:T(8,128)(2,1)S(1)}, bf16[16,256]{1,0:T(8,128)(2,1)S(1)}, bf16[16,256]{1,0:T(8,128)(2,1)S(1)}, bf16[16,256]{1,0:T(8,1...) fusion(bf16[128,16,256]{0,2,1:T(8,128)(2,1)S(1)} %bitcast.336), kind=kLoop, calls=%fused_computation.69 | loop fusion | bytes 311296 | tf_op jit(solution)/shard_map/split | solution.py:79
  82.4 12.4 %slice_reduce_fusion.19 = (bf16[16,256]{1,0:T(8,128)(2,1)S(1)}, bf16[16,256]{1,0:T(8,128)(2,1)S(1)}, bf16[16,256]{1,0:T(8,128)(2,1)S(1)}, bf16[16,256]{1,0:T(8,1...) fusion(bf16[128,16,256]{0,2,1:T(8,128)(2,1)S(1)} %bitcast.337), kind=kLoop, calls=%fused_computation.50 | loop fusion | bytes 311296 | tf_op jit(solution)/shard_map/split | solution.py:79
  94.8 12.6 %slice_reduce_fusion = (bf16[16,256]{1,0:T(8,128)(2,1)S(1)}, bf16[16,256]{1,0:T(8,128)(2,1)S(1)}, bf16[16,256]{1,0:T(8,128)(2,1)S(1)}, bf16[16,256]{1,0:T(8,128)...) fusion(bf16[128,16,256]{0,2,1:T(8,128)(2,1)S(1)} %bitcast.338), kind=kLoop, calls=%fused_computation.31 | loop fusion | bytes 311296 | tf_op jit(solution)/shard_map/split | solution.py:79
  183.5 14.3 %all-to-all-start = ((bf16[128,1,16,256]{3,2,1,0:T(8,128)(2,1)}), bf16[128,1,16,256]{3,2,1,0:T(8,128)(2,1)S(1)}, u32[]{:S(2)}, u32[]{:S(2)}) async-start(bf16[128,1,16,256]{3,2,1,0:T(8,128)(2,1)} %constant_dynamic-update-slice_fusion), calls=%async_computation | async-start | bytes 2097152 | tf_op jit(solution)/shard_map/all_to_all | solution.py:79
  199.5 52.1 %all-to-all-done = bf16[128,1,16,256]{3,2,1,0:T(8,128)(2,1)S(1)} async-done(((bf16[128,1,16,256]{3,2,1,0:T(8,128)(2,1)}), bf16[128,1,16,256]{3,2,1,0:T(8,128)(2,1)S(1)}, u32[]{:S(2)}, u32[]{:S(2)}) %all-to-all-start) | async-done | bytes 1048608 | tf_op jit(solution)/shard_map/all_to_all | solution.py:79
  251.9 1.5 fusion.31
  254.2 37.6 %while.17 = (s32[]{:T(128)}, f32[1,1024]{1,0:T(1,128)S(1)}, f32[1,1024]{1,0:T(1,128)S(1)}, f32[1,1024,128]{2,1,0:T(8,128)S(1)}, s32[17]{0:T(128)S(1)}, /*index=5...) while((s32[]{:T(128)}, f32[1,1024]{1,0:T(1,128)S(1)}, ...), condition=%wide.region_4.5_spmd.clone, body=%wide.region_1.4_spmd.clone.sunk | while | flops 68562176 | bytes 3024009 | solution.py:131
  254.3 0.7 dynamic_slice.38
  254.9 0.7 add_add_fusion.2
  256.5 0.7 dynamic_slice.38
  257.1 0.7 add_add_fusion.2
  258.7 0.7 dynamic_slice.38
  259.4 0.7 add_add_fusion.2
  260.9 0.7 dynamic_slice.38
  261.6 0.7 add_add_fusion.2
  263.1 0.7 dynamic_slice.38
  263.8 0.7 add_add_fusion.2
  265.3 0.7 dynamic_slice.38
  266.0 0.7 add_add_fusion.2
  267.5 0.7 dynamic_slice.38
  268.2 0.7 add_add_fusion.2
  269.8 0.7 dynamic_slice.38
  270.4 0.7 add_add_fusion.2
  272.6 0.7 add_add_fusion.2
  274.2 0.7 dynamic_slice.38
  274.9 0.7 add_add_fusion.2
  276.4 0.7 dynamic_slice.38
  277.1 0.7 add_add_fusion.2
  278.6 0.7 dynamic_slice.38
  279.3 0.7 add_add_fusion.2
  280.8 0.7 dynamic_slice.38
  281.5 0.7 add_add_fusion.2
  283.0 0.7 dynamic_slice.38
  283.7 0.7 add_add_fusion.2
  285.9 0.7 add_add_fusion.2
  287.5 0.7 dynamic_slice.38
  288.1 0.7 add_add_fusion.2
  289.7 0.7 dynamic_slice.38
  290.4 0.7 add_add_fusion.2
  292.1 0.9 select_convert_fusion
  (288 shorter events, 94.3 us)
Async XLA Ops:
  183.5 14.4 %copy-start.2 = (bf16[1,128,128]{2,1,0:T(8,128)(2,1)S(1)}, bf16[1,128,128]{2,1,0:T(8,128)(2,1)}, u32[]{:S(2)}) copy-start(bf16[1,128,128]{2,1,0:T(8,128)(2,1)} %param.11) | copy-start | bytes 98308
  183.5 14.9 %copy-start = (bf16[8,128,128]{2,1,0:T(8,128)(2,1)S(1)}, bf16[8,128,128]{2,1,0:T(8,128)(2,1)}, u32[]{:S(2)}) copy-start(bf16[8,128,128]{2,1,0:T(8,128)(2,1)} %param.10) | copy-start | bytes 786436
  183.5 68.1 %all-to-all-start = ((bf16[128,1,16,256]{3,2,1,0:T(8,128)(2,1)}), bf16[128,1,16,256]{3,2,1,0:T(8,128)(2,1)S(1)}, u32[]{:S(2)}, u32[]{:S(2)}) async-start(bf16[128,1,16,256]{3,2,1,0:T(8,128)(2,1)} %constant_dynamic-update-slice_fusion), calls=%async_computation | async-start | bytes 2097152 | tf_op jit(solution)/shard_map/all_to_all | solution.py:79
  197.8 0.7 copy-start.3
  253.4 0.8 copy-start.1
